TPU v7x, 32 devices: a whole 2x2x4 slice. The times are simulated.
32 devices in a mesh: group: 2 (over x), wide: 16 (over z, y, core).
Axes of the slice: x: 2, y: 2, z: 4, core: 2. Of those that a mesh axis runs over, the one named last changes fastest.
Arguments:
- tokens: bfloat16 [32, 18432], P('group', 'wide'), parts along dimension 0, may hold values from -6 to 6
- norm_gain: float32 [18432], P('wide'), may hold values from 0.1 to 1.9
- w_query: bfloat16 [18432, 12288], P('wide'), may hold values from -0.046875 to 0.046875
- w_keyval: bfloat16 [18432, 512], P('wide'), may hold values from -0.046875 to 0.046875
- w_out: bfloat16 [12288, 18432], P(None, 'wide'), may hold values from -0.0546875 to 0.0546875
- cache: bfloat16 [32, 4096, 512], P(('group', 'wide')), parts along dimension 0, may hold values from -1000 to 1000, as said below
- lengths: int32 [32], P(('group', 'wide')), parts along dimension 0, may hold values from 256 to 4096, as said below
Outputs:
- hidden: bfloat16 [32, 18432], P('group', 'wide'), parts along dimension 0
- fresh: bfloat16 [32, 1, 512], P(('group', 'wide')), parts along dimension 0
There are 2 independent parts, one for each index of `group`. A program takes and returns all parts, laid end to end along the dimension named above; an argument that names none is the same for every part. Nothing has to cross between parts.
Inputs may be any that keep to these rules, and one draw needn't show every extreme that they name: `lengths`: every row's length lies between 256 and 4096; some row has length exactly 4096 and some row exactly 256. `cache`: finite entries.
All inputs are finite; a program needn't handle non-finite values.
Results may differ from a plain program's by a relative error of at most 0.0059.
Values may be sent and summed in bfloat16 or wider, within the bound.
A program may use at most 128 MiB of HBM per device.

v0:
```python
import jax
import jax.numpy as jnp
from jax import lax
from jax.sharding import PartitionSpec as P

D = 18432
STEPS = 1


def masked_scores(heads_q, keys, valid, factor):
    scores = jnp.einsum("rhd,rld->rhl", heads_q, keys, preferred_element_type=jnp.float32) * factor
    return jnp.where(valid, scores, -1e30)


def attend(query, cache, fresh, lengths, step):
    own = query.shape[0]
    head = fresh.shape[2] // 2
    heads = query.shape[1] // head
    factor = head ** (-0.5)
    heads_q = query.reshape(own, heads, head)
    new_valid = (jnp.arange(fresh.shape[1]) <= step)[None, None, :]
    new_scores = masked_scores(heads_q, fresh[:, :, :head], new_valid, factor)
    new_top = jnp.max(new_scores, axis=2)
    old_valid = (jnp.arange(cache.shape[1])[None, :] < lengths[:, None])[:, None, :]
    old_scores = masked_scores(heads_q, cache[:, :, :head], old_valid, factor)
    top = jnp.maximum(jnp.max(old_scores, axis=2), new_top)
    old_exp = jnp.where(old_valid, jnp.exp(old_scores - top[..., None]), 0.0)
    total = jnp.sum(old_exp, axis=2)
    summed = jnp.einsum(
        "rhl,rld->rhd",
        old_exp.astype(jnp.bfloat16),
        cache[:, :, head:],
        preferred_element_type=jnp.float32,
    )
    new_exp = jnp.where(new_valid, jnp.exp(new_scores - top[..., None]), 0.0)
    total = total + jnp.sum(new_exp, axis=2)
    summed = summed + jnp.einsum(
        "rhs,rsd->rhd",
        new_exp.astype(jnp.bfloat16),
        fresh[:, :, head:],
        preferred_element_type=jnp.float32,
    )
    return (summed / total[..., None]).reshape(own, heads * head).astype(jnp.bfloat16)


def row_total(sumsq_part):
    return lax.psum(sumsq_part, "wide")


def on_device(tokens, norm_gain, w_query, w_keyval, w_out, cache, lengths):
    count = lax.axis_size("wide")
    own = tokens.shape[0] // count
    base_row = lax.axis_index("wide") * own
    query_width = w_query.shape[1]
    weights = jnp.concatenate([w_query, w_keyval], axis=1)
    state = tokens.astype(jnp.float32)
    fresh = jnp.zeros((own, STEPS, w_keyval.shape[1]), jnp.bfloat16)
    sumsq_part = jnp.sum(state * state, axis=1)
    scaled_in = (state * norm_gain[None, :]).astype(jnp.bfloat16)
    sumsq = lax.dynamic_slice_in_dim(row_total(sumsq_part), base_row, own, 0)

    def project(start, rows, source=scaled_in):
        return jnp.dot(source, weights, preferred_element_type=jnp.float32)

    projected = lax.psum_scatter(
        project(jnp.int32(0), own * lax.axis_size("wide")), "wide", scatter_dimension=0, tiled=True
    )
    scale = lax.rsqrt(sumsq / D + 1e-06)
    projected = projected * scale[:, None]
    query = projected[:, :query_width].astype(jnp.bfloat16)
    keyval = projected[:, query_width:].astype(jnp.bfloat16)
    fresh = fresh.at[:, 0].set(keyval)
    attended = attend(query, cache, fresh, lengths, 0)
    state = state + jnp.dot(
        lax.all_gather(attended, "wide", axis=0, tiled=True),
        w_out,
        preferred_element_type=jnp.float32,
    )
    return (state.astype(jnp.bfloat16), fresh)


def solution(mesh):
    in_specs = (
        P("group", "wide"),
        P("wide"),
        P("wide", None),
        P("wide", None),
        P(None, "wide"),
        P(("group", "wide"), None, None),
        P(("group", "wide")),
    )
    out_specs = (P("group", "wide"), P(("group", "wide"), None, None))
    return jax.shard_map(
        on_device, mesh=mesh, in_specs=in_specs, out_specs=out_specs, check_vma=False
    )
```

profile of v0, /device:TPU:1, one launch (start us, length us, event | category | flops | bytes accessed | tf_op | source)
XLA Modules:
  0.0 167.5 jit_solution(13738991732101839401)
XLA Ops:
  7.2 0.0 copy-start.2
  7.2 0.0 copy-start
  7.2 0.0 all-reduce.3.cloned.1.call-start
  7.2 17.2 %fusion = f32[16,12800]{1,0:T(8,128)} fusion(bf16[1152,512]{1,0:T(8,128)(2,1)} %param.12, bf16[1152,12288]{1,0:T(8,128)(2,1)} %param.11, bf16[16,1152]{1,0:T(8,128)(2,1)} %param.9, f32[1152]{0:T(1024)} %param.10), kind=kOutput, calls=%fused_computation | convolution fusion | flops 530896896 | bytes 30351872 | tf_op jit(solution)/shard_map/dot_general | solution.py:63
  24.4 0.0 all-reduce.3.cloned.1.call-update
  24.5 0.0 copy-done
  24.5 0.1 fusion.30
  24.6 30.7 %psum.7 = f32[16]{0:T(128)S(1)} all-reduce(f32[16]{0:T(128)S(1)} %fusion.30), channel_id=1, replica_groups=mesh['group'=2,'wide'=16] {'wide'}, use_global_device_ids=true, to_apply=%region_2.0 | all-reduce | flops 16 | bytes 128 | tf_op jit(solution)/shard_map/psum | solution.py:47
  55.3 0.6 dynamic_slice.3
  57.2 0.0 copy-done.2
  57.2 0.6 dynamic-slice.7
  57.8 61.0 %all-reduce.3.cloned.1.call-done = f32[16,12800]{1,0:T(8,128)} async-done(((f32[16,12800]{1,0:T(8,128)}), f32[16,12800]{1,0:T(8,128)}) %all-reduce.3.cloned.1.call-update) | async-done | bytes 819216
  118.8 1.7 %fusion.31 = bf16[1,12800]{1,0:T(2,128)(2,1)S(1)} fusion(f32[16,12800]{1,0:T(8,128)} %all-reduce.3.cloned.1.call-done, u32[]{:T(128)} %bitcast.7, f32[]{:T(128)} %bitcast.1), kind=kLoop, calls=%fused_computation.31 | loop fusion | flops 25600 | bytes 76808 | tf_op jit(solution)/shard_map/convert.5
  120.5 0.1 slice_reduce_fusion
  120.7 0.0 copy-start.1
  120.7 2.4 %fusion.37 = (f32[48]{0:T(128)S(1)}, f32[48,4096]{1,0:T(8,128)S(1)}) fusion(bf16[48,256]{1,0:T(8,128)(2,1)S(1)} %reshape.142, bf16[1,4096,512]{2,1,0:T(8,128)(2,1)} %param.14, pred[4096]{0:T(1024)(128)(4,1)S(1)} %iota_compare_fusion), kind=kOutput, calls=%fused_computation.43 | convolution fusion | flops 101253072 | bytes 2912448 | tf_op jit(solution)/shard_map/rhd,rld->rhl/dot_general | solution.py:11
  123.2 0.1 convert_convert_fusion
  123.3 0.3 fusion.21
  123.7 2.1 %fusion.17 = bf16[48,256]{1,0:T(8,128)(2,1)S(1)} fusion(bf16[1,4096,512]{2,1,0:T(8,128)(2,1)} %param.14, f32[48,4096]{1,0:T(8,128)S(1)} %get-tuple-element.17, f32[48]{0:T(128)S(1)} %get-tuple-element.15, pred[4096]{0:T(1024)(128)(4,1)S(1)} %iota_compare_fusion, f32[48]{0:T(128)S(1)} %fusion.36, f32[256]{0:T(256)S(1)} %bitcast.36, f32[48]{0:T(128)S(1)} %get-tuple-element.14), kind=kOutput, calls=%fused_computation.15 | convolution fusion | flops 101302272 | bytes 2913856 | tf_op jit(solution)/shard_map/rhl,rld->rhd/dot_general | solution.py:29
  125.8 23.1 %all-gather = bf16[16,1,12288]{2,1,0:T(2,128)(2,1)S(1)} all-gather(bf16[1,1,12288]{2,1,0:T(2,128)(2,1)S(1)} %reshape.148), channel_id=1, replica_groups=mesh['group'=2,'wide'=16] {'wide'}, dimensions={0}, use_global_device_ids=true | all-gather | bytes 417792 | tf_op jit(solution)/shard_map/all_gather | solution.py:75
  148.9 11.8 %fusion.5 = bf16[16,1152]{1,0:T(8,128)(2,1)} fusion(bf16[12288,1152]{1,0:T(8,128)(2,1)} %param.13, bf16[16,1,12288]{2,1,0:T(2,128)(2,1)S(1)} %all-gather, bf16[16,1152]{1,0:T(8,128)(2,1)S(1)} %copy-done), kind=kOutput, calls=%fused_computation.7 | convolution fusion | flops 453040128 | bytes 28778496 | tf_op jit(solution)/shard_map/dot_general | solution.py:74
  160.7 0.0 copy-done.1
  (6 shorter events, 0.1 us)
Async XLA Ops:
  7.2 50.0 %copy-start.2 = (u32[32]{0:T(128)S(1)}, u32[32]{0:T(128)}, u32[]{:S(2)}) copy-start(u32[32]{0:T(128)} %constant.53) | copy-start | bytes 388
  7.2 17.3 %copy-start = (bf16[16,1152]{1,0:T(8,128)(2,1)S(1)}, bf16[16,1152]{1,0:T(8,128)(2,1)}, u32[]{:S(2)}) copy-start(bf16[16,1152]{1,0:T(8,128)(2,1)} %param.9) | copy-start | bytes 110596
  7.2 111.6 %all-reduce.3.cloned.1.call-start = ((), (), s32[]{:S(2)}) async-start(), calls=%async_computation | async-start | bytes 1638400
  120.7 40.0 %copy-start.1 = (bf16[1,1,512]{2,1,0:T(2,128)(2,1)}, bf16[1,1,512]{2,1,0:T(2,128)(2,1)S(1)}, u32[]{:S(2)}) copy-start(bf16[1,1,512]{2,1,0:T(2,128)(2,1)S(1)} %slice_bitcast_fusion) | copy-start | bytes 3076
Sparse Core Ops, SparseCore 0:
  24.6 94.1 all-reduce.2
where the time goes:
time: 168 us
  waiting for transfers between devices  61 us (36%)
  blocking collectives  53.7 us (32%)
  matrix products  33.7 us (20%)
  between operations  15.5 us (9%)
  other arithmetic  2.19 us (1%)
    unnamed x2, waiting for transfers between devices  61 us
    psum x1, blocking collectives, row_total(): return lax.psum(sumsq_part, 'wide')  30.7 us
    all_gather x1, blocking collectives, on_device(): lax.all_gather(attended, 'wide', axis=0, tiled=True)  23.1 us
    dot_general x1, matrix products, project(): return jnp.dot(source, weights, preferred_element_type=jnp.float32)  17.2 us
    dot_general x1, matrix products, on_device(): jnp.dot(lax.all_gather(attended, 'wide', axis=0, tiled=True), w_out, pref...  11.8 us
  transfers between devices with their start and end apart: 1, of which 1 were waited for; matrix products, arithmetic and copies ran while one was open for 1% of the time, Pallas kernels for 0%

commit v1 on v0

v1 whole, which is shorter than its diff:
```python
import functools

import jax
import jax.numpy as jnp
from jax import lax
from jax.experimental import pallas as pl
from jax.experimental.pallas import tpu as pltpu
from jax.sharding import PartitionSpec as P

MESH = pl.DeviceIdType.MESH
F32 = jnp.float32
BF16 = jnp.bfloat16
HEAD = 256
HALF = 128
GROUP = 8
SLOTS = 3
OUT_PIECES = 6


def layer_kernel(
    eps, factor, chips,
    len_ref, tokens_ref, gain_ref, wq_ref, wkv_ref, wo_ref, cache_ref,
    hidden_ref, fresh_ref,
    scaled, wq_buf, wkv_buf, wo_buf, cache_buf,
    part, pair_send, pair_recv, sums, far_send, far_recv,
    kv_part, kv_pair_send, kv_pair_recv, kv_sums, kv_far_send, kv_far_recv,
    query, gathered, wide32,
    wq_sem, wkv_sem, wo_sem, cache_sem,
    pair_ssem, pair_rsem, far_ssem, far_rsem,
    row_ssem, row_rsem, twin_ssem, twin_rsem,
):
    rows, width = tokens_ref.shape
    chunks = wq_ref.shape[1] // (GROUP * HEAD)
    heads = wq_ref.shape[1] // HEAD
    piece = wo_ref.shape[0] // OUT_PIECES
    me = lax.axis_index("wide")
    chip, core = me // 2, me % 2
    twin = chip * 2 + 1 - core

    def peer(d):
        return lax.rem(chip + d, chips)

    def row_piece(r):
        return pl.ds(pl.multiple_of(r * 2 * GROUP, 2 * GROUP), 2 * GROUP)

    def wq_copy(j):
        return pltpu.make_async_copy(
            wq_ref.at[:, pl.ds(j * GROUP * HEAD, GROUP * HEAD)], wq_buf.at[j % SLOTS], wq_sem.at[j % SLOTS]
        )

    def wo_copy(i):
        at = pl.ds(i * piece, piece)
        return pltpu.make_async_copy(wo_ref.at[at], wo_buf.at[at], wo_sem.at[i])

    wkv_copy = pltpu.make_async_copy(wkv_ref, wkv_buf, wkv_sem)
    cache_copy = pltpu.make_async_copy(cache_ref.at[0], cache_buf, cache_sem)

    wkv_copy.start()
    for j in range(SLOTS):
        wq_copy(j).start()

    barrier = pltpu.get_barrier_semaphore()
    pl.semaphore_signal(barrier, inc=1, device_id={"wide": twin}, device_id_type=MESH)
    for d in range(1, chips):
        pl.semaphore_signal(barrier, inc=1, device_id={"wide": peer(d) * 2 + core}, device_id_type=MESH)

    state = tokens_ref[...].astype(F32)
    sumsq = jnp.sum(state * state, axis=1, keepdims=True)
    scaled[...] = (state * gain_ref[...]).astype(BF16)
    pl.semaphore_wait(barrier, chips)

    def pair_copy(s):
        if s == 0:
            src, dst = kv_pair_send, kv_pair_recv
        else:
            src, dst = pair_send.at[s - 1], pair_recv.at[s - 1]
        return pltpu.make_async_remote_copy(
            src_ref=src, dst_ref=dst, send_sem=pair_ssem.at[s], recv_sem=pair_rsem.at[s],
            device_id={"wide": twin}, device_id_type=MESH,
        )

    def far_copy(s, d):
        if s == 0:
            src, dst = kv_far_send.at[d - 1], kv_far_recv.at[d - 1]
        else:
            src, dst = far_send.at[s - 1, d - 1], far_recv.at[s - 1, d - 1]
        return pltpu.make_async_remote_copy(
            src_ref=src, dst_ref=dst, send_sem=far_ssem.at[s, d - 1], recv_sem=far_rsem.at[s, d - 1],
            device_id={"wide": peer(d) * 2 + core}, device_id_type=MESH,
        )

    def combine(s):
        pair_copy(s).wait_recv()
        if s == 0:
            kv_sums[...] = kv_part[:, core] + kv_pair_recv[...]
            for d in range(1, chips):
                kv_far_send[d - 1] = kv_sums[peer(d)]
        else:
            for k in range(chips):
                sums[s - 1, k] = part[s - 1, row_piece(2 * k + core), :] + pair_recv[s - 1, k].astype(F32)
            for d in range(1, chips):
                far_send[s - 1, d - 1] = sums[s - 1, peer(d)].astype(BF16)
        for d in range(1, chips):
            far_copy(s, d).start()

    wkv_copy.wait()
    keyval = jnp.dot(scaled[...], wkv_buf[...], preferred_element_type=F32)
    for r in range(rows):
        at = (r // 2, r % 2)
        for n in range(4):
            kv_part[at[0], at[1], n : n + 1, :] = keyval[r : r + 1, n * HALF : (n + 1) * HALF]
        kv_part[at[0], at[1], 4:5, :] = jnp.broadcast_to(sumsq[r : r + 1], (1, HALF))
        kv_part[at[0], at[1], 5:8, :] = jnp.zeros((3, HALF), F32)
    kv_pair_send[...] = kv_part[:, 1 - core]
    pair_copy(0).start()

    for j in range(chunks):
        slot = j % SLOTS
        wq_copy(j).wait()

        def project(h, carry, slot=slot, j=j):
            at = pl.ds(pl.multiple_of(h * HEAD, HEAD), HEAD)
            got = jnp.dot(scaled[...], wq_buf[slot, :, at], preferred_element_type=F32)
            part[j, pl.ds(h, rows, stride=2 * GROUP), :] = got[:, :HALF]
            part[j, pl.ds(h + GROUP, rows, stride=2 * GROUP), :] = got[:, HALF:]
            return carry

        lax.fori_loop(0, GROUP, project, 0)
        if j + SLOTS < chunks:
            wq_copy(j + SLOTS).start()
        elif j + SLOTS == chunks:
            cache_copy.start()
            for i in range(OUT_PIECES):
                wo_copy(i).start()
        for k in range(chips):
            pair_send[j, k] = part[j, row_piece(2 * k + 1 - core), :].astype(BF16)
        pair_copy(j + 1).start()
        combine(j)
    combine(chunks)

    for d in range(1, chips):
        far_copy(0, d).wait_recv()
    total = kv_sums[chip]
    for d in range(1, chips):
        total = total + kv_far_recv[d - 1]
    scale = lax.rsqrt(total[4:5, :1] / (width * 2 * chips) + eps)
    keyval = (total[0:4] * scale).astype(BF16).astype(F32)
    fresh_ref[...] = keyval
    for j in range(chunks):
        for d in range(1, chips):
            far_copy(j + 1, d).wait_recv()
        mine = sums[j, chip]
        for d in range(1, chips):
            mine = mine + far_recv[j, d - 1].astype(F32)
        query[j * GROUP : (j + 1) * GROUP, :HALF] = mine[:GROUP]
        query[j * GROUP : (j + 1) * GROUP, HALF:] = mine[GROUP:]

    heads_q = (query[...] * scale).astype(BF16)
    new_key = jnp.concatenate([keyval[0:1], keyval[1:2]], axis=1)
    new_value = jnp.concatenate([keyval[2:3], keyval[3:4]], axis=1)
    new_score = jnp.sum(heads_q.astype(F32) * new_key, axis=1, keepdims=True) * factor
    cache_copy.wait()
    scores = lax.dot_general(
        heads_q, cache_buf[:, :HEAD], (((1,), (1,)), ((), ())), preferred_element_type=F32
    ) * factor
    valid = lax.broadcasted_iota(jnp.int32, scores.shape, 1) < len_ref[0]
    scores = jnp.where(valid, scores, -1e30)
    top = jnp.maximum(jnp.max(scores, axis=1, keepdims=True), new_score)
    exps = jnp.where(valid, jnp.exp(scores - top), 0.0)
    new_exp = jnp.exp(new_score - top)
    norm = jnp.sum(exps, axis=1, keepdims=True) + new_exp
    summed = jnp.dot(exps.astype(BF16), cache_buf[:, HEAD:], preferred_element_type=F32)
    summed = summed + new_exp.astype(BF16).astype(F32) * new_value
    gathered[me] = (summed / norm).astype(BF16)

    def row_copy(d):
        return pltpu.make_async_remote_copy(
            src_ref=gathered.at[me], dst_ref=gathered.at[me],
            send_sem=row_ssem.at[d - 1], recv_sem=row_rsem.at[d - 1],
            device_id={"wide": peer(d) * 2 + core}, device_id_type=MESH,
        )

    def twin_copy(d):
        at = peer(d) * 2 + core
        return pltpu.make_async_remote_copy(
            src_ref=gathered.at[at], dst_ref=gathered.at[at],
            send_sem=twin_ssem.at[d], recv_sem=twin_rsem.at[d],
            device_id={"wide": twin}, device_id_type=MESH,
        )

    for d in range(1, chips):
        row_copy(d).start()
    twin_copy(0).start()
    for d in range(chips - 1, 0, -1):
        row_copy(d).wait_recv()
        twin_copy(chips - d).start()
    for d in range(chips):
        twin_copy(d).wait_recv()

    wide32[0] = gathered[:, :, :HALF].astype(F32).reshape(rows * heads, HALF)
    wide32[1] = gathered[:, :, HALF:].astype(F32).reshape(rows * heads, HALF)

    def output(h, acc):
        at = pl.ds(h, rows, stride=heads)
        low = wide32[0, at, :].astype(BF16)
        high = wide32[1, at, :].astype(BF16)
        lhs = jnp.concatenate([low, high], axis=1)
        rhs = wo_buf[pl.ds(pl.multiple_of(h * HEAD, HEAD), HEAD), :]
        return acc + jnp.dot(lhs, rhs, preferred_element_type=F32)

    acc = tokens_ref[...].astype(F32)
    per = heads // OUT_PIECES
    for i in range(OUT_PIECES):
        wo_copy(i).wait()
        acc = lax.fori_loop(i * per, (i + 1) * per, output, acc)
    hidden_ref[...] = acc.astype(BF16)

    for s in range(chunks + 1):
        pair_copy(s).wait_send()
        for d in range(1, chips):
            far_copy(s, d).wait_send()
    for d in range(1, chips):
        row_copy(d).wait_send()
    for d in range(chips):
        twin_copy(d).wait_send()


def fused(lengths, tokens, norm_gain, w_query, w_keyval, w_out, cache):
    count = lax.axis_size("wide")
    chips = count // 2
    rows, width = tokens.shape
    heads = w_query.shape[1] // HEAD
    chunks = heads // GROUP
    positions = cache.shape[1]
    vmem = pl.BlockSpec(memory_space=pltpu.VMEM)
    hbm = pl.BlockSpec(memory_space=pl.ANY)
    dma = pltpu.SemaphoreType.DMA
    kernel = functools.partial(layer_kernel, 1e-06, HEAD ** (-0.5), chips)
    hidden, keyval = pl.pallas_call(
        kernel,
        out_shape=(
            jax.ShapeDtypeStruct((rows, width), BF16),
            jax.ShapeDtypeStruct((4, HALF), F32),
        ),
        in_specs=[pl.BlockSpec(memory_space=pltpu.SMEM), vmem, vmem, hbm, hbm, hbm, hbm],
        out_specs=(vmem, vmem),
        scratch_shapes=[
            pltpu.VMEM((rows, width), BF16),
            pltpu.VMEM((SLOTS, width, GROUP * HEAD), BF16),
            pltpu.VMEM(w_keyval.shape, BF16),
            pltpu.VMEM(w_out.shape, BF16),
            pltpu.VMEM(cache.shape[1:], BF16),
            pltpu.VMEM((chunks, rows * 2 * GROUP, HALF), F32),
            pltpu.VMEM((chunks, chips, 2 * GROUP, HALF), BF16),
            pltpu.VMEM((chunks, chips, 2 * GROUP, HALF), BF16),
            pltpu.VMEM((chunks, chips, 2 * GROUP, HALF), F32),
            pltpu.VMEM((chunks, chips - 1, 2 * GROUP, HALF), BF16),
            pltpu.VMEM((chunks, chips - 1, 2 * GROUP, HALF), BF16),
            pltpu.VMEM((chips, 2, 8, HALF), F32),
            pltpu.VMEM((chips, 8, HALF), F32),
            pltpu.VMEM((chips, 8, HALF), F32),
            pltpu.VMEM((chips, 8, HALF), F32),
            pltpu.VMEM((chips - 1, 8, HALF), F32),
            pltpu.VMEM((chips - 1, 8, HALF), F32),
            pltpu.VMEM((heads, HEAD), F32),
            pltpu.VMEM((rows, heads, HEAD), BF16),
            pltpu.VMEM((2, rows * heads, HALF), F32),
            dma((SLOTS,)), dma, dma((OUT_PIECES,)), dma,
            dma((chunks + 1,)), dma((chunks + 1,)),
            dma((chunks + 1, chips - 1)), dma((chunks + 1, chips - 1)),
            dma((chips - 1,)), dma((chips - 1,)), dma((chips,)), dma((chips,)),
        ],
        compiler_params=pltpu.CompilerParams(
            collective_id=0, has_side_effects=True, vmem_limit_bytes=60 * 1024 * 1024
        ),
        cost_estimate=pl.CostEstimate(
            flops=2 * rows * width * (w_query.shape[1] * 2) + 4 * w_query.shape[1] * positions,
            bytes_accessed=2 * (w_query.size + w_out.size + cache.size),
            transcendentals=heads * positions,
        ),
    )(lengths, tokens, norm_gain[None, :], w_query, w_keyval, w_out, cache)
    return hidden, keyval.reshape(1, 1, 4 * HALF).astype(BF16)


def masked_scores(heads_q, keys, valid, factor):
    scores = jnp.einsum("rhd,rld->rhl", heads_q, keys, preferred_element_type=F32) * factor
    return jnp.where(valid, scores, -1e30)


def attend(query, cache, fresh, lengths):
    own = query.shape[0]
    head = fresh.shape[2] // 2
    heads = query.shape[1] // head
    factor = head ** (-0.5)
    heads_q = query.reshape(own, heads, head)
    new_scores = masked_scores(heads_q, fresh[:, :, :head], True, factor)
    old_valid = (jnp.arange(cache.shape[1])[None, :] < lengths[:, None])[:, None, :]
    old_scores = masked_scores(heads_q, cache[:, :, :head], old_valid, factor)
    top = jnp.maximum(jnp.max(old_scores, axis=2), jnp.max(new_scores, axis=2))
    old_exp = jnp.where(old_valid, jnp.exp(old_scores - top[..., None]), 0.0)
    new_exp = jnp.exp(new_scores - top[..., None])
    total = jnp.sum(old_exp, axis=2) + jnp.sum(new_exp, axis=2)
    summed = jnp.einsum("rhl,rld->rhd", old_exp.astype(BF16), cache[:, :, head:], preferred_element_type=F32)
    summed = summed + jnp.einsum(
        "rhs,rsd->rhd", new_exp.astype(BF16), fresh[:, :, head:], preferred_element_type=F32
    )
    return (summed / total[..., None]).reshape(own, heads * head).astype(BF16)


def plain(lengths, tokens, norm_gain, w_query, w_keyval, w_out, cache):
    count = lax.axis_size("wide")
    own = tokens.shape[0] // count
    base_row = lax.axis_index("wide") * own
    state = tokens.astype(F32)
    scaled_in = (state * norm_gain[None, :]).astype(BF16)
    sumsq = lax.psum(jnp.sum(state * state, axis=1), "wide")
    sumsq = lax.dynamic_slice_in_dim(sumsq, base_row, own, 0)
    scale = lax.rsqrt(sumsq / (tokens.shape[1] * count) + 1e-06)[:, None]

    def project(weights):
        partial = jnp.dot(scaled_in, weights, preferred_element_type=F32)
        return (lax.psum_scatter(partial, "wide", scatter_dimension=0, tiled=True) * scale).astype(BF16)

    query = project(w_query)
    fresh = project(w_keyval)[:, None, :]
    attended = attend(query, cache, fresh, lengths)
    everything = lax.all_gather(attended, "wide", axis=0, tiled=True)
    state = state + jnp.dot(everything, w_out, preferred_element_type=F32)
    return state.astype(BF16), fresh


def on_device(tokens, norm_gain, w_query, w_keyval, w_out, cache, lengths):
    count = lax.axis_size("wide")
    fits = (
        tokens.shape[0] == count
        and count <= 16
        and tokens.shape[1] % HALF == 0
        and w_out.size + cache.size <= 18 * 1024 * 1024
    )
    body = fused if fits else plain
    return body(lengths, tokens, norm_gain, w_query, w_keyval, w_out, cache)


def solution(mesh):
    in_specs = (
        P("group", "wide"),
        P("wide"),
        P("wide", None),
        P("wide", None),
        P(None, "wide"),
        P(("group", "wide"), None, None),
        P(("group", "wide")),
    )
    out_specs = (P("group", "wide"), P(("group", "wide"), None, None))
    return jax.shard_map(
        on_device, mesh=mesh, in_specs=in_specs, out_specs=out_specs, check_vma=False
    )
```

time: 168 us -> 49.6 us (0.30)
  waiting for transfers between devices: 61 us -> 0 us
  blocking collectives: 53.7 us -> 0 us
  Pallas kernels: 0 us -> 44.1 us
  matrix products: 33.7 us -> 0 us
  between operations: 15.5 us -> 1.29 us
  local copies, waits for them, and re-layouts: 1.36 us -> 3.27 us
    unnamed x2 -> x0, waiting for transfers between devices: 61 us -> none
    pallas_call x0 -> x1, Pallas kernels: none -> 44.1 us  [fused(): pl.pallas_call(kernel, out_shape=(jax.ShapeDtypeStruct((rows, width), BF1...]
    dot_general x5 -> x0, matrix products: 33.7 us -> none  [the longest x1 17.2 us: project(): return jnp.dot(source, weights, preferred_element_type=jnp.float32)]
    psum x1 -> x0, blocking collectives: 30.7 us -> none  [row_total(): return lax.psum(sumsq_part, 'wide')]
    all_gather x1 -> x0, blocking collectives: 23.1 us -> none  [on_device(): lax.all_gather(attended, 'wide', axis=0, tiled=True)]
    another operation x2 -> x0, other arithmetic: 1.71 us -> none
  transfers between devices with their start and end apart: 1 -> 0, of which waited for: 1 -> 0; matrix products, arithmetic and copies ran while one was open for 1% -> 0% of each run, Pallas kernels for 0% -> 0%
where the time goes in v1:
time: 49.6 us; the launch traced here: 49.3 us
  Pallas kernels  44.1 us (89%)
  local copies, waits for them, and re-layouts  3.27 us (7%)
  between operations  1.29 us (3%)
  other arithmetic  0.66 us (1%)
    pallas_call x1, Pallas kernels, fused(): pl.pallas_call(kernel, out_shape=(jax.ShapeDtypeStruct((rows, width), BF1...  44.1 us
    unnamed x1, local copies, waits for them, and re-layouts  1.39 us
    broadcast_in_dim x1, local copies, waits for them, and re-layouts, fused(): norm_gain[None, :]  1.29 us

profile of v1, /device:TPU:1, one launch (start us, length us, event | category | flops | bytes accessed | tf_op | source)
XLA Modules:
  0.0 49.3 jit_solution(18225188717923805482)
XLA Ops:
  1.3 1.3 %broadcast_in_dim.3.gain_ref = f32[1,1152]{1,0:T(1,128)} reshape(f32[1152]{0:T(1024)} %param.8) | data formatting | bytes 9216 | tf_op jit(solution)/shard_map/broadcast_in_dim | solution.py:281
  2.6 44.1 %shard_map.86 = (bf16[16,1152]{1,0:T(8,128)(2,1)}, f32[4,128]{1,0:T(4,128)}) custom-call(s32[1]{0:T(128)S(6)} %copy.10.len_ref, bf16[16,1152]{1,0:T(8,128)(2,1)} %tokens_ref.1, f32[1,1152]{1,0:T(1,128)} %broadcast_in_dim.3.gain_ref, bf16[1152,12288]{1,0:T(8,128)(2,1)} %wq_ref.1, bf16[1152,512]{1,0:T(8,128)(2,1)} %wkv_ref.1, bf16[12288,1152]{1,0:T(8,128)(2,1)} %wo_ref.1, ...), custom_call_target="tpu_custom_call" | custom-call | flops 1107296256 | bytes 60817408 | tf_op jit(solution)/shard_map/pallas_call | solution.py:239
  46.6 0.7 %convert_element_type.14 = bf16[4,128]{1,0:T(4,128)(2,1)S(1)} convert(f32[4,128]{1,0:T(4,128)} %get-tuple-element.5) | non-fusion elementwise | flops 512 | bytes 3072 | tf_op jit(solution)/shard_map/convert_element_type | solution.py:282
  47.3 0.6 %convert_element_type.15 = bf16[1,1,512]{2,1,0:T(2,128)(2,1)} reshape(bf16[4,128]{1,0:T(4,128)(2,1)S(1)} %convert_element_type.14) | data formatting | bytes 2048 | tf_op jit(solution)/shard_map/convert_element_type | solution.py:282
  47.9 1.4 %copy.11 = bf16[16,1152]{1,0:T(8,128)(2,1)} copy(bf16[16,1152]{1,0:T(8,128)(2,1)} %get-tuple-element.8) | data formatting | bytes 73728

commit v2 on v1

--- a/solution.py
+++ b/solution.py
@@ -13,8 +13,11 @@
 HEAD = 256
 HALF = 128
 GROUP = 8
+PAIR = 2
+TEAM = PAIR * GROUP
 SLOTS = 3
 OUT_PIECES = 6
+COLUMNS = 4 * HEAD
 
 
 def layer_kernel(
@@ -24,21 +27,25 @@
     scaled, wq_buf, wkv_buf, wo_buf, cache_buf,
     part, pair_send, pair_recv, sums, far_send, far_recv,
     kv_part, kv_pair_send, kv_pair_recv, kv_sums, kv_far_send, kv_far_recv,
-    query, gathered, wide32,
+    gathered, wide32,
     wq_sem, wkv_sem, wo_sem, cache_sem,
     pair_ssem, pair_rsem, far_ssem, far_rsem,
     row_ssem, row_rsem, twin_ssem, twin_rsem,
 ):
     rows, width = tokens_ref.shape
     chunks = wq_ref.shape[1] // (GROUP * HEAD)
-    heads = wq_ref.shape[1] // HEAD
     piece = wo_ref.shape[0] // OUT_PIECES
     me = lax.axis_index("wide")
     chip, core = me // 2, me % 2
     twin = chip * 2 + 1 - core
 
     def peer(d):
-        return lax.rem(chip + d, chips)
+        found, bit = 0, 1
+        while bit < chips:
+            own = (chip // bit) % 2
+            found = found + bit * (1 - own if d & bit else own)
+            bit *= 2
+        return found
 
     def row_piece(r):
         return pl.ds(pl.multiple_of(r * 2 * GROUP, 2 * GROUP), 2 * GROUP)
@@ -66,7 +73,9 @@
 
     state = tokens_ref[...].astype(F32)
     sumsq = jnp.sum(state * state, axis=1, keepdims=True)
-    scaled[...] = (state * gain_ref[...]).astype(BF16)
+    for n in range(width // HALF):
+        at = slice(n * HALF, (n + 1) * HALF)
+        scaled[:, at] = (state[:, at] * gain_ref[n : n + 1, :]).astype(BF16)
     pl.semaphore_wait(barrier, chips)
 
     def pair_copy(s):
@@ -100,7 +109,7 @@
                 sums[s - 1, k] = part[s - 1, row_piece(2 * k + core), :] + pair_recv[s - 1, k].astype(F32)
             for d in range(1, chips):
                 far_send[s - 1, d - 1] = sums[s - 1, peer(d)].astype(BF16)
-        for d in range(1, chips):
+        for d in range(chips - 1, 0, -1):
             far_copy(s, d).start()
 
     wkv_copy.wait()
@@ -114,115 +123,148 @@
     kv_pair_send[...] = kv_part[:, 1 - core]
     pair_copy(0).start()
 
+    def project(j):
+        slot = j % SLOTS
+
+        def columns(n, carry):
+            at = pl.ds(pl.multiple_of(n * COLUMNS, COLUMNS), COLUMNS)
+            got = jnp.dot(scaled[...], wq_buf[slot, :, at], preferred_element_type=F32)
+            for i in range(COLUMNS // HEAD):
+                h = n * (COLUMNS // HEAD) + i
+                low = got[:, i * HEAD : i * HEAD + HALF]
+                high = got[:, i * HEAD + HALF : (i + 1) * HEAD]
+                part[j, pl.ds(h, rows, stride=2 * GROUP), :] = low
+                part[j, pl.ds(h + GROUP, rows, stride=2 * GROUP), :] = high
+            return carry
+
+        lax.fori_loop(0, GROUP * HEAD // COLUMNS, columns, 0)
+
+    def own_sums():
+        for d in range(1, chips):
+            far_copy(0, d).wait_recv()
+        total = kv_sums[chip]
+        for d in range(1, chips):
+            total = total + kv_far_recv[d - 1]
+        scale = lax.rsqrt(total[4:5, :1] / (width * 2 * chips) + eps)
+        keyval = (total[0:4] * scale).astype(BF16)
+        for n in range(4):
+            fresh_ref[0, :, n * HALF : (n + 1) * HALF] = keyval[n : n + 1]
+        keyval = keyval.astype(F32)
+        new_key = jnp.concatenate([keyval[0:1], keyval[1:2]], axis=1)
+        new_value = jnp.concatenate([keyval[2:3], keyval[3:4]], axis=1)
+        return scale, new_key, new_value
+
+    def own_query(j):
+        for d in range(1, chips):
+            far_copy(j + 1, d).wait_recv()
+        mine = sums[j, chip]
+        for d in range(1, chips):
+            mine = mine + far_recv[j, d - 1].astype(F32)
+        return jnp.concatenate([mine[:GROUP], mine[GROUP:]], axis=1)
+
+    def attention(g):
+        scale, new_key, new_value = new_token
+        heads_q = jnp.concatenate([own_query(g * PAIR + i) for i in range(PAIR)], axis=0)
+        heads_q = (heads_q * scale).astype(BF16)
+        new_score = jnp.sum(heads_q.astype(F32) * new_key, axis=1, keepdims=True) * factor
+        scores = lax.dot_general(
+            heads_q, cache_buf[:, :HEAD], (((1,), (1,)), ((), ())), preferred_element_type=F32
+        ) * factor
+        valid = lax.broadcasted_iota(jnp.int32, scores.shape, 1) < len_ref[0]
+        scores = jnp.where(valid, scores, -1e30)
+        top = jnp.maximum(jnp.max(scores, axis=1, keepdims=True), new_score)
+        exps = jnp.where(valid, jnp.exp(scores - top), 0.0)
+        new_exp = jnp.exp(new_score - top)
+        norm = jnp.sum(exps, axis=1, keepdims=True) + new_exp
+        summed = jnp.dot(exps.astype(BF16), cache_buf[:, HEAD:], preferred_element_type=F32)
+        summed = summed + new_exp.astype(BF16).astype(F32) * new_value
+        gathered[g, me] = (summed / norm).astype(BF16)
+        for d in range(chips - 1, 0, -1):
+            row_copy(g, d).start()
+        twin_copy(g, 0).start()
+
+    def row_copy(g, d):
+        return pltpu.make_async_remote_copy(
+            src_ref=gathered.at[g, me], dst_ref=gathered.at[g, me],
+            send_sem=row_ssem.at[g, d - 1], recv_sem=row_rsem.at[g, d - 1],
+            device_id={"wide": peer(d) * 2 + core}, device_id_type=MESH,
+        )
+
+    def twin_copy(g, d):
+        at = peer(d) * 2 + core
+        return pltpu.make_async_remote_copy(
+            src_ref=gathered.at[g, at], dst_ref=gathered.at[g, at],
+            send_sem=twin_ssem.at[g, d], recv_sem=twin_rsem.at[g, d],
+            device_id={"wide": twin}, device_id_type=MESH,
+        )
+
+    def share(g):
+        for d in range(1, chips):
+            row_copy(g, d).wait_recv()
+            twin_copy(g, d).start()
+
+    def output(g, acc):
+        for d in range(chips):
+            twin_copy(g, d).wait_recv()
+        wide32[0] = gathered[g, :, :, :HALF].astype(F32).reshape(rows * TEAM, HALF)
+        wide32[1] = gathered[g, :, :, HALF:].astype(F32).reshape(rows * TEAM, HALF)
+        per = OUT_PIECES // teams
+        count = COLUMNS // HEAD
+
+        def step(n, acc):
+            sides = []
+            for i in range(count):
+                at = pl.ds(n * count + i, rows, stride=TEAM)
+                sides.append(wide32[0, at, :].astype(BF16))
+                sides.append(wide32[1, at, :].astype(BF16))
+            lhs = jnp.concatenate(sides, axis=1)
+            at = pl.ds(pl.multiple_of(g * TEAM * HEAD + n * COLUMNS, COLUMNS), COLUMNS)
+            return acc + jnp.dot(lhs, wo_buf[at, :], preferred_element_type=F32)
+
+        steps = TEAM * HEAD // COLUMNS
+        for i in range(per):
+            wo_copy(g * per + i).wait()
+            acc = lax.fori_loop(i * steps // per, (i + 1) * steps // per, step, acc)
+        return acc
+
+    teams = chunks // PAIR
     for j in range(chunks):
-        slot = j % SLOTS
         wq_copy(j).wait()
-
-        def project(h, carry, slot=slot, j=j):
-            at = pl.ds(pl.multiple_of(h * HEAD, HEAD), HEAD)
-            got = jnp.dot(scaled[...], wq_buf[slot, :, at], preferred_element_type=F32)
-            part[j, pl.ds(h, rows, stride=2 * GROUP), :] = got[:, :HALF]
-            part[j, pl.ds(h + GROUP, rows, stride=2 * GROUP), :] = got[:, HALF:]
-            return carry
-
-        lax.fori_loop(0, GROUP, project, 0)
+        project(j)
         if j + SLOTS < chunks:
             wq_copy(j + SLOTS).start()
+            if j == 0:
+                cache_copy.start()
         elif j + SLOTS == chunks:
-            cache_copy.start()
             for i in range(OUT_PIECES):
                 wo_copy(i).start()
         for k in range(chips):
             pair_send[j, k] = part[j, row_piece(2 * k + 1 - core), :].astype(BF16)
         pair_copy(j + 1).start()
         combine(j)
+        if j == PAIR + 2:
+            new_token = own_sums()
+            cache_copy.wait()
+            attention(0)
     combine(chunks)
-
-    for d in range(1, chips):
-        far_copy(0, d).wait_recv()
-    total = kv_sums[chip]
-    for d in range(1, chips):
-        total = total + kv_far_recv[d - 1]
-    scale = lax.rsqrt(total[4:5, :1] / (width * 2 * chips) + eps)
-    keyval = (total[0:4] * scale).astype(BF16).astype(F32)
-    fresh_ref[...] = keyval
-    for j in range(chunks):
-        for d in range(1, chips):
-            far_copy(j + 1, d).wait_recv()
-        mine = sums[j, chip]
-        for d in range(1, chips):
-            mine = mine + far_recv[j, d - 1].astype(F32)
-        query[j * GROUP : (j + 1) * GROUP, :HALF] = mine[:GROUP]
-        query[j * GROUP : (j + 1) * GROUP, HALF:] = mine[GROUP:]
-
-    heads_q = (query[...] * scale).astype(BF16)
-    new_key = jnp.concatenate([keyval[0:1], keyval[1:2]], axis=1)
-    new_value = jnp.concatenate([keyval[2:3], keyval[3:4]], axis=1)
-    new_score = jnp.sum(heads_q.astype(F32) * new_key, axis=1, keepdims=True) * factor
-    cache_copy.wait()
-    scores = lax.dot_general(
-        heads_q, cache_buf[:, :HEAD], (((1,), (1,)), ((), ())), preferred_element_type=F32
-    ) * factor
-    valid = lax.broadcasted_iota(jnp.int32, scores.shape, 1) < len_ref[0]
-    scores = jnp.where(valid, scores, -1e30)
-    top = jnp.maximum(jnp.max(scores, axis=1, keepdims=True), new_score)
-    exps = jnp.where(valid, jnp.exp(scores - top), 0.0)
-    new_exp = jnp.exp(new_score - top)
-    norm = jnp.sum(exps, axis=1, keepdims=True) + new_exp
-    summed = jnp.dot(exps.astype(BF16), cache_buf[:, HEAD:], preferred_element_type=F32)
-    summed = summed + new_exp.astype(BF16).astype(F32) * new_value
-    gathered[me] = (summed / norm).astype(BF16)
-
-    def row_copy(d):
-        return pltpu.make_async_remote_copy(
-            src_ref=gathered.at[me], dst_ref=gathered.at[me],
-            send_sem=row_ssem.at[d - 1], recv_sem=row_rsem.at[d - 1],
-            device_id={"wide": peer(d) * 2 + core}, device_id_type=MESH,
-        )
-
-    def twin_copy(d):
-        at = peer(d) * 2 + core
-        return pltpu.make_async_remote_copy(
-            src_ref=gathered.at[at], dst_ref=gathered.at[at],
-            send_sem=twin_ssem.at[d], recv_sem=twin_rsem.at[d],
-            device_id={"wide": twin}, device_id_type=MESH,
-        )
-
-    for d in range(1, chips):
-        row_copy(d).start()
-    twin_copy(0).start()
-    for d in range(chips - 1, 0, -1):
-        row_copy(d).wait_recv()
-        twin_copy(chips - d).start()
-    for d in range(chips):
-        twin_copy(d).wait_recv()
-
-    wide32[0] = gathered[:, :, :HALF].astype(F32).reshape(rows * heads, HALF)
-    wide32[1] = gathered[:, :, HALF:].astype(F32).reshape(rows * heads, HALF)
-
-    def output(h, acc):
-        at = pl.ds(h, rows, stride=heads)
-        low = wide32[0, at, :].astype(BF16)
-        high = wide32[1, at, :].astype(BF16)
-        lhs = jnp.concatenate([low, high], axis=1)
-        rhs = wo_buf[pl.ds(pl.multiple_of(h * HEAD, HEAD), HEAD), :]
-        return acc + jnp.dot(lhs, rhs, preferred_element_type=F32)
-
     acc = tokens_ref[...].astype(F32)
-    per = heads // OUT_PIECES
-    for i in range(OUT_PIECES):
-        wo_copy(i).wait()
-        acc = lax.fori_loop(i * per, (i + 1) * per, output, acc)
+    for g in range(1, teams):
+        attention(g)
+        share(g - 1)
+        acc = output(g - 1, acc)
+    share(teams - 1)
+    acc = output(teams - 1, acc)
     hidden_ref[...] = acc.astype(BF16)
 
     for s in range(chunks + 1):
         pair_copy(s).wait_send()
         for d in range(1, chips):
             far_copy(s, d).wait_send()
-    for d in range(1, chips):
-        row_copy(d).wait_send()
-    for d in range(chips):
-        twin_copy(d).wait_send()
+    for g in range(teams):
+        for d in range(1, chips):
+            row_copy(g, d).wait_send()
+        for d in range(chips):
+            twin_copy(g, d).wait_send()
 
 
 def fused(lengths, tokens, norm_gain, w_query, w_keyval, w_out, cache):
@@ -231,16 +273,17 @@
     rows, width = tokens.shape
     heads = w_query.shape[1] // HEAD
     chunks = heads // GROUP
+    teams = chunks // PAIR
     positions = cache.shape[1]
     vmem = pl.BlockSpec(memory_space=pltpu.VMEM)
     hbm = pl.BlockSpec(memory_space=pl.ANY)
     dma = pltpu.SemaphoreType.DMA
     kernel = functools.partial(layer_kernel, 1e-06, HEAD ** (-0.5), chips)
-    hidden, keyval = pl.pallas_call(
+    hidden, fresh = pl.pallas_call(
         kernel,
         out_shape=(
             jax.ShapeDtypeStruct((rows, width), BF16),
-            jax.ShapeDtypeStruct((4, HALF), F32),
+            jax.ShapeDtypeStruct((1, 1, 4 * HALF), BF16),
         ),
         in_specs=[pl.BlockSpec(memory_space=pltpu.SMEM), vmem, vmem, hbm, hbm, hbm, hbm],
         out_specs=(vmem, vmem),
@@ -262,13 +305,12 @@
             pltpu.VMEM((chips, 8, HALF), F32),
             pltpu.VMEM((chips - 1, 8, HALF), F32),
             pltpu.VMEM((chips - 1, 8, HALF), F32),
-            pltpu.VMEM((heads, HEAD), F32),
-            pltpu.VMEM((rows, heads, HEAD), BF16),
-            pltpu.VMEM((2, rows * heads, HALF), F32),
+            pltpu.VMEM((teams, rows, TEAM, HEAD), BF16),
+            pltpu.VMEM((2, rows * TEAM, HALF), F32),
             dma((SLOTS,)), dma, dma((OUT_PIECES,)), dma,
             dma((chunks + 1,)), dma((chunks + 1,)),
             dma((chunks + 1, chips - 1)), dma((chunks + 1, chips - 1)),
-            dma((chips - 1,)), dma((chips - 1,)), dma((chips,)), dma((chips,)),
+            dma((teams, chips - 1)), dma((teams, chips - 1)), dma((teams, chips)), dma((teams, chips)),
         ],
         compiler_params=pltpu.CompilerParams(
             collective_id=0, has_side_effects=True, vmem_limit_bytes=60 * 1024 * 1024
@@ -278,8 +320,8 @@
             bytes_accessed=2 * (w_query.size + w_out.size + cache.size),
             transcendentals=heads * positions,
         ),
-    )(lengths, tokens, norm_gain[None, :], w_query, w_keyval, w_out, cache)
-    return hidden, keyval.reshape(1, 1, 4 * HALF).astype(BF16)
+    )(lengths, tokens, norm_gain.reshape(width // HALF, HALF), w_query, w_keyval, w_out, cache)
+    return hidden, fresh
 
 
 def masked_scores(heads_q, keys, valid, factor):
@@ -333,7 +375,7 @@
     count = lax.axis_size("wide")
     fits = (
         tokens.shape[0] == count
-        and count <= 16
+        and count in (4, 8, 16)
         and tokens.shape[1] % HALF == 0
         and w_out.size + cache.size <= 18 * 1024 * 1024
     )

time: 49.6 us -> 38.4 us (0.77)
  Pallas kernels: 44.1 us -> 34.2 us
  other arithmetic: 0.66 us -> 0 us
  local copies, waits for them, and re-layouts: 3.27 us -> 2.62 us
    pallas_call x1, Pallas kernels: 44.1 us -> 34.2 us  [fused(): pl.pallas_call(kernel, out_shape=(jax.ShapeDtypeStruct((rows, width), BF1...]
    broadcast_in_dim x1 -> x0, local copies, waits for them, and re-layouts: 1.29 us -> none  [fused(): norm_gain[None, :]]
    unnamed x1 -> x2, local copies, waits for them, and re-layouts: 1.39 us -> 2.62 us
    convert_element_type x1 -> x0, other arithmetic: 0.66 us -> none  [fused(): return (hidden, keyval.reshape(1, 1, 4 * HALF).astype(BF16))]
    convert_element_type x1 -> x0, local copies, waits for them, and re-layouts: 0.59 us -> none  [fused(): return (hidden, keyval.reshape(1, 1, 4 * HALF).astype(BF16))]
where the time goes in v2:
time: 38.4 us; the launch traced here: 38.1 us
  Pallas kernels  34.2 us (89%)
  local copies, waits for them, and re-layouts  2.62 us (7%)
  between operations  1.29 us (3%)
    pallas_call x1, Pallas kernels, fused(): pl.pallas_call(kernel, out_shape=(jax.ShapeDtypeStruct((rows, width), BF1...  34.2 us
    unnamed x2, local copies, waits for them, and re-layouts  2.62 us

profile of v2, /device:TPU:1, one launch (start us, length us, event | category | flops | bytes accessed | tf_op | source)
XLA Modules:
  0.0 38.1 jit_solution(17432361773812308303)
XLA Ops:
  1.3 34.2 %shard_map.86 = (bf16[16,1152]{1,0:T(8,128)(2,1)}, bf16[1,1,512]{2,1,0:T(2,128)(2,1)}) custom-call(s32[1]{0:T(128)S(6)} %copy.11.len_ref, bf16[16,1152]{1,0:T(8,128)(2,1)} %tokens_ref.1, f32[9,128]{1,0:T(8,128)} %bitcast.1, bf16[1152,12288]{1,0:T(8,128)(2,1)} %wq_ref.1, bf16[1152,512]{1,0:T(8,128)(2,1)} %wkv_ref.1, bf16[12288,1152]{1,0:T(8,128)(2,1)} %wo_ref.1, ...), custom_call_target="tpu_custom_call" | custom-call | flops 1107296256 | bytes 60817408 | tf_op jit(solution)/shard_map/pallas_call | solution.py:282
  35.5 1.4 %copy.12 = bf16[16,1152]{1,0:T(8,128)(2,1)} copy(bf16[16,1152]{1,0:T(8,128)(2,1)} %get-tuple-element.4) | data formatting | bytes 73728
  36.9 1.2 %copy.13 = bf16[1,1,512]{2,1,0:T(2,128)(2,1)} copy(bf16[1,1,512]{2,1,0:T(2,128)(2,1)} %get-tuple-element.5) | data formatting | bytes 2048

commit v3 on v2

--- a/solution.py
+++ b/solution.py
@@ -27,7 +27,7 @@
     scaled, wq_buf, wkv_buf, wo_buf, cache_buf,
     part, pair_send, pair_recv, sums, far_send, far_recv,
     kv_part, kv_pair_send, kv_pair_recv, kv_sums, kv_far_send, kv_far_recv,
-    gathered, wide32,
+    gathered, wide32, keys_t,
     wq_sem, wkv_sem, wo_sem, cache_sem,
     pair_ssem, pair_rsem, far_ssem, far_rsem,
     row_ssem, row_rsem, twin_ssem, twin_rsem,
@@ -167,9 +167,7 @@
         heads_q = jnp.concatenate([own_query(g * PAIR + i) for i in range(PAIR)], axis=0)
         heads_q = (heads_q * scale).astype(BF16)
         new_score = jnp.sum(heads_q.astype(F32) * new_key, axis=1, keepdims=True) * factor
-        scores = lax.dot_general(
-            heads_q, cache_buf[:, :HEAD], (((1,), (1,)), ((), ())), preferred_element_type=F32
-        ) * factor
+        scores = jnp.dot(heads_q, keys_t[...], preferred_element_type=F32) * factor
         valid = lax.broadcasted_iota(jnp.int32, scores.shape, 1) < len_ref[0]
         scores = jnp.where(valid, scores, -1e30)
         top = jnp.maximum(jnp.max(scores, axis=1, keepdims=True), new_score)
@@ -245,13 +243,15 @@
         if j == PAIR + 2:
             new_token = own_sums()
             cache_copy.wait()
+            keys_t[...] = cache_buf[:, :HEAD].T
             attention(0)
     combine(chunks)
     acc = tokens_ref[...].astype(F32)
     for g in range(1, teams):
         attention(g)
         share(g - 1)
-        acc = output(g - 1, acc)
+    for g in range(teams - 1):
+        acc = output(g, acc)
     share(teams - 1)
     acc = output(teams - 1, acc)
     hidden_ref[...] = acc.astype(BF16)
@@ -307,6 +307,7 @@
             pltpu.VMEM((chips - 1, 8, HALF), F32),
             pltpu.VMEM((teams, rows, TEAM, HEAD), BF16),
             pltpu.VMEM((2, rows * TEAM, HALF), F32),
+            pltpu.VMEM((HEAD, positions), BF16),
             dma((SLOTS,)), dma, dma((OUT_PIECES,)), dma,
             dma((chunks + 1,)), dma((chunks + 1,)),
             dma((chunks + 1, chips - 1)), dma((chunks + 1, chips - 1)),

time: 38.4 us -> 37.3 us (0.971)
  Pallas kernels: 34.2 us -> 33.1 us
    pallas_call x1, Pallas kernels: 34.2 us -> 33.1 us  [fused(): pl.pallas_call(kernel, out_shape=(jax.ShapeDtypeStruct((rows, width), BF1...]
where the time goes in v3:
time: 37.3 us; the launch traced here: 37 us
  Pallas kernels  33.1 us (89%)
  local copies, waits for them, and re-layouts  2.62 us (7%)
  between operations  1.29 us (3%)
    pallas_call x1, Pallas kernels, fused(): pl.pallas_call(kernel, out_shape=(jax.ShapeDtypeStruct((rows, width), BF1...  33.1 us
    unnamed x2, local copies, waits for them, and re-layouts  2.62 us

profile of v3, /device:TPU:1, one launch (start us, length us, event | category | flops | bytes accessed | tf_op | source)
XLA Modules:
  0.0 37.0 jit_solution(2088711506718561189)
XLA Ops:
  1.3 33.1 %shard_map.86 = (bf16[16,1152]{1,0:T(8,128)(2,1)}, bf16[1,1,512]{2,1,0:T(2,128)(2,1)}) custom-call(s32[1]{0:T(128)S(6)} %copy.11.len_ref, bf16[16,1152]{1,0:T(8,128)(2,1)} %tokens_ref.1, f32[9,128]{1,0:T(8,128)} %bitcast.1, bf16[1152,12288]{1,0:T(8,128)(2,1)} %wq_ref.1, bf16[1152,512]{1,0:T(8,128)(2,1)} %wkv_ref.1, bf16[12288,1152]{1,0:T(8,128)(2,1)} %wo_ref.1, ...), custom_call_target="tpu_custom_call" | custom-call | flops 1107296256 | bytes 60817408 | tf_op jit(solution)/shard_map/pallas_call | solution.py:282
  34.4 1.4 %copy.12 = bf16[16,1152]{1,0:T(8,128)(2,1)} copy(bf16[16,1152]{1,0:T(8,128)(2,1)} %get-tuple-element.4) | data formatting | bytes 73728
  35.8 1.2 %copy.13 = bf16[1,1,512]{2,1,0:T(2,128)(2,1)} copy(bf16[1,1,512]{2,1,0:T(2,128)(2,1)} %get-tuple-element.5) | data formatting | bytes 2048
